TPU v7x, 32 devices: a whole 2x2x4 slice. The times are simulated.
32 devices in a mesh: groups: 1, tm: 8 (over z, y), expert: 2 (over x), head: 2 (over core).
Axes of the slice: x: 2, y: 2, z: 4, core: 2. Of those that a mesh axis runs over, the one named last changes fastest.
Arguments:
- queries: bfloat16 [2, 1024, 2048], P(('groups', 'expert'), 'tm', 'head'), may hold values from -40 to 40
- keys: bfloat16 [2, 1024, 256], P(('groups', 'expert'), 'tm', 'head'), may hold values from -4.5 to 4.5
- values: bfloat16 [2, 1024, 256], P(('groups', 'expert'), 'tm', 'head'), may hold values from -12 to 12
- segments: int32 [2, 1024], P(('groups', 'expert')), may hold values from 0 to 31, never falling along the last dimension, each value on 1 to 128 neighbouring positions
- resid: bfloat16 [2, 1024, 2048], P(('groups', 'expert'), 'tm', 'head'), may hold values from -6 to 6
- output_weight: bfloat16 [2048, 2048], P('head', 'expert'), may hold values from -0.375 to 0.375
- norm_gain: float32 [2048], P('head'), may hold values from 0.5 to 1.5
- routes: int32 [2, 1024, 8], P(('groups', 'expert'), 'tm'), may hold values from 0 to 15, all different within a row; in each aligned block of 128 rows (0 to 127, 128 to 255, ..., all dimensions but the last counted through in order) at most 96 rows name the same one
- route_weights: float32 [2, 1024, 8], P(('groups', 'expert'), 'tm'), may hold values from 0.05 to 0.3
- w_gu: bfloat16 [16, 2048, 768], P(('tm', 'expert'), 'head'), may hold values from -0.125 to 0.125
- w_down: bfloat16 [16, 384, 2048], P(('tm', 'expert'), None, 'head'), may hold values from -0.3125 to 0.3125
Outputs:
- layer_out: bfloat16 [2, 1024, 2048], P(('groups', 'expert'), 'tm', 'head')
Inputs may be any that keep to these rules, and one draw needn't show every extreme that they name: `routes`: each row names 8 different experts; among the 128 positions of one device's aligned block no expert is named more than 96 times, a bound that some block reaches. `segments`: segment numbers never fall along a sequence; every segment holds 1 to 128 positions.
All inputs are finite; a program needn't handle non-finite values.
Results may differ from a plain program's by a relative error of at most 0.012.
Values may be sent and summed in bfloat16 or wider, within the bound.
A program may use at most 64 MiB of HBM per device.

v0:
```python
import math

import jax
import jax.numpy as jnp
from jax import lax
from jax.sharding import PartitionSpec as P

masked_score = -1e30
epsilon = 1e-06


def deliver(buffer):
    return lax.all_to_all(buffer, ("tm", "expert"), split_axis=0, concat_axis=0, tiled=True)


def local(
    queries,
    keys,
    values,
    segments,
    resid,
    output_weight,
    norm_gain,
    routes,
    route_weights,
    w_gu,
    w_down,
):
    head_size = keys.shape[2]
    tokens = queries.shape[1]
    groups = queries.shape[2] // head_size
    query_blk = queries[0].reshape(tokens, groups, head_size)
    seq_ids = segments[0]
    query_ids = lax.dynamic_slice_in_dim(seq_ids, lax.axis_index("tm") * tokens, tokens)
    score_scale = 1.0 / math.sqrt(head_size)
    running = jnp.full((groups, tokens), masked_score, jnp.float32)
    key_blk = lax.all_gather(keys, "tm", axis=1, tiled=True)[0]
    value_blk = lax.all_gather(values, "tm", axis=1, tiled=True)[0]
    scores = (
        jnp.einsum("tgd,nd->gtn", query_blk, key_blk, preferred_element_type=jnp.float32)
        * score_scale
    )
    allowed = seq_ids[None, None, :] <= query_ids[None, :, None]
    scores = jnp.where(allowed, scores, masked_score)
    newmax = jnp.maximum(running, jnp.max(scores, axis=-1))
    exp_scores = jnp.where(allowed, jnp.exp(scores - newmax[..., None]), 0.0)
    total = jnp.sum(exp_scores, axis=-1)
    weighted = jnp.einsum(
        "gtn,nd->gtd",
        exp_scores.astype(jnp.bfloat16),
        value_blk,
        preferred_element_type=jnp.float32,
    )
    running, total, weighted = (newmax, total, weighted)
    attended = (
        (weighted / total[..., None])
        .transpose(1, 0, 2)
        .reshape(tokens, groups * head_size)
        .astype(jnp.bfloat16)
    )
    partial_value = jnp.dot(
        attended,
        lax.all_gather(output_weight, "expert", axis=1, tiled=True),
        preferred_element_type=jnp.float32,
    )
    width = resid.shape[2]
    full_width = partial_value.shape[1]
    offset = lax.axis_index("head") * width
    placed = lax.dynamic_update_slice_in_dim(
        jnp.zeros((tokens, full_width), jnp.float32), resid[0].astype(jnp.float32), offset, 1
    )
    hidden_in = lax.psum((partial_value + placed).astype(jnp.bfloat16), "head").astype(jnp.float32)
    inv_rms = lax.rsqrt(jnp.mean(hidden_in * hidden_in, axis=-1) + epsilon)
    hidden_half = lax.dynamic_slice_in_dim(hidden_in, offset, width, 1)
    normed_half = (hidden_half * inv_rms[:, None] * norm_gain).astype(jnp.bfloat16)
    expert_total = lax.axis_size("tm") * lax.axis_size("expert")
    top_count = routes.shape[2]
    capacity = min(tokens, 3 * tokens * top_count // (2 * expert_total))
    flat_routes = routes[0].reshape(-1)
    flat_weights = route_weights[0].reshape(-1)
    onehot = (flat_routes[:, None] == jnp.arange(expert_total, dtype=jnp.int32)[None, :]).astype(
        jnp.int32
    )
    earlier = jnp.cumsum(onehot, axis=0) - onehot
    rank = jnp.sum(earlier * onehot, axis=1)
    slot_ids = flat_routes * capacity + rank
    slot_range = jnp.arange(expert_total * capacity, dtype=jnp.int32)
    pair_match = slot_range[:, None] == slot_ids[None, :]
    dispatch = jnp.sum(
        pair_match.reshape(expert_total * capacity, tokens, top_count).astype(jnp.float32), axis=2
    )
    send_rows = jnp.dot(
        dispatch.astype(jnp.bfloat16), normed_half, preferred_element_type=jnp.float32
    ).astype(jnp.bfloat16)
    arrived = deliver(send_rows.reshape(expert_total, capacity, width))
    arrived_rows = arrived.reshape(expert_total * capacity, width)
    block_gate = jnp.dot(arrived_rows, w_gu[0], preferred_element_type=jnp.float32).astype(
        jnp.bfloat16
    )
    gate_up = lax.psum(block_gate, "head").astype(jnp.float32)
    feedforward_count = w_down.shape[1]
    activated = (
        jax.nn.silu(gate_up[:, :feedforward_count]) * gate_up[:, feedforward_count:]
    ).astype(jnp.bfloat16)
    expert_out = jnp.dot(activated, w_down[0], preferred_element_type=jnp.float32).astype(
        jnp.bfloat16
    )
    returned = deliver(expert_out.reshape(expert_total, capacity, width))
    returned_rows = returned.reshape(expert_total * capacity, width).astype(jnp.float32)
    combine = jnp.sum(
        (pair_match.astype(jnp.float32) * flat_weights[None, :]).reshape(
            expert_total * capacity, tokens, top_count
        ),
        axis=2,
    )
    mixed = jnp.dot(combine.T, returned_rows, precision=lax.Precision.HIGHEST)
    layer_out = (hidden_half + mixed).astype(jnp.bfloat16)
    return layer_out[None]


def solution(mesh):
    placed = (
        P(("groups", "expert"), "tm", "head"),
        P(("groups", "expert"), "tm", "head"),
        P(("groups", "expert"), "tm", "head"),
        P(("groups", "expert"), None),
        P(("groups", "expert"), "tm", "head"),
        P("head", "expert"),
        P("head"),
        P(("groups", "expert"), "tm", None),
        P(("groups", "expert"), "tm", None),
        P(("tm", "expert"), "head", None),
        P(("tm", "expert"), None, "head"),
    )
    return jax.shard_map(
        local,
        mesh=mesh,
        in_specs=placed,
        out_specs=P(("groups", "expert"), "tm", "head"),
        check_vma=False,
    )
```

profile of v0, /device:TPU:0, one launch (start us, length us, event | category | flops | bytes accessed | tf_op | source)
XLA Modules:
  0.0 298.3 jit_solution(2646855066966801977)
XLA Ops:
  6.5 0.0 copy-start
  6.5 0.0 all-gather.2.cloned.1.call-start
  6.5 0.7 all-gather.2.cloned.1.call-update
  7.3 0.0 all-reduce.3.cloned.1.call-start
  7.3 0.8 copy.31
  8.1 0.1 eq.45
  8.2 0.1 eq.41
  8.3 4.5 %reduce-window.6 = s32[16,8,128]{2,1,0:T(8,128)S(1)} reduce-window(s32[16,8,128]{2,1,0:T(8,128)S(1)} %fusion.33, s32[]{:T(128)} %constant.15.clone.1), window={size=1x1x128 pad=0_0x0_0x127_0}, to_apply=%region_3.4 | reduce-window | flops 2080768 | bytes 131076 | tf_op jit(solution)/shard_map/reduce-window
  12.8 0.1 slice.16
  12.9 0.1 copy.34
  13.1 0.1 copy.35
  13.1 0.1 broadcast_add_fusion
  13.3 0.1 reduce_sum.49
  13.4 1.0 copy.38
  14.4 0.9 copy.29
  15.2 0.7 fusion.35
  15.9 32.9 %all_gather.9 = bf16[1,1024,128]{2,1,0:T(8,128)(2,1)S(1)} all-gather(bf16[1,128,128]{2,1,0:T(8,128)(2,1)} %param.12), channel_id=1, replica_groups=mesh['groups'=1,'tm'=8,'expert'=2,'head'=2] {'tm'}, dimensions={1}, use_global_device_ids=true | all-gather | bytes 294912 | tf_op jit(solution)/shard_map/all_gather | solution.py:37
  48.8 26.4 %all_gather.10 = bf16[1,1024,128]{1,2,0:T(8,128)(2,1)S(1)} all-gather(bf16[1,128,128]{1,2,0:T(8,128)(2,1)S(1)} %copy.29), channel_id=1, replica_groups=mesh['groups'=1,'tm'=8,'expert'=2,'head'=2] {'tm'}, dimensions={1}, use_global_device_ids=true | all-gather | bytes 294912 | tf_op jit(solution)/shard_map/all_gather | solution.py:38
  75.2 0.0 copy-done.3
  75.3 0.2 broadcast_compare_fusion
  75.5 0.8 fusion
  76.2 1.0 fusion.1
  77.3 1.2 fusion.18
  78.4 0.0 copy-start.1
  78.4 0.0 all-gather.2.cloned.1.call-done
  78.5 0.0 copy-start.2
  78.5 3.0 fusion.40
  81.5 0.0 copy-done.1
  81.5 0.0 copy-start.4
  81.5 0.1 fusion.22
  81.6 0.9 convert_element_type.62
  82.5 0.0 all-reduce.3.cloned.1.call-update
  82.5 0.0 all-reduce.5.cloned.1.call-start
  82.6 0.0 copy-done.2
  82.6 8.4 %convert_reduce_fusion = (bf16[1536,128]{1,0:T(8,128)(2,1)}, f32[1536,128]{1,0:T(8,128)S(1)}) fusion(s32[128,8]{0,1:T(8,128)S(1)} %copy.36, f32[128,8]{0,1:T(8,128)S(1)} %bitcast.92), kind=kLoop, calls=%fused_computation | loop fusion | flops 7471104 | bytes 1187840 | tf_op jit(solution)/shard_map/reduce_sum | solution.py:89
  91.0 9.7 %all-reduce.3.cloned.1.call-done = bf16[128,2048]{1,0:T(8,128)(2,1)} async-done(((bf16[128,2048]{1,0:T(8,128)(2,1)}), bf16[128,2048]{1,0:T(8,128)(2,1)}) %all-reduce.3.cloned.1.call-update) | async-done | bytes 524304 | tf_op jit(solution)/shard_map/psum | solution.py:72
  100.6 1.2 multiply_reduce_fusion
  101.9 1.1 convert_element_type.63
  103.0 2.0 convolution_convert_fusion
  105.1 78.3 %all_to_all.10 = bf16[16,96,1024]{2,1,0:T(8,128)(2,1)S(1)} all-to-all(bf16[16,96,1024]{2,1,0:T(8,128)(2,1)S(1)} %bitcast.84), channel_id=1, replica_groups=mesh['groups'=1,'tm'=8,'expert'=2,'head'=2] {'tm','expert'}, dimensions={0} | all-to-all | bytes 6291456 | tf_op jit(solution)/shard_map/all_to_all | solution.py:13
  183.3 0.0 copy-done
  183.3 3.8 %convolution_convert_fusion.2 = bf16[1536,768]{1,0:T(8,128)(2,1)} fusion(bf16[1536,1024]{1,0:T(8,128)(2,1)S(1)} %bitcast.85, bf16[1,1024,768]{2,1,0:T(8,128)(2,1)S(1)} %copy-done), kind=kOutput, calls=%fused_computation.8 | convolution fusion | flops 2417098752 | bytes 7077888 | tf_op jit(solution)/shard_map/dot_general | solution.py:97
  187.1 0.0 all-reduce.5.cloned.1.call-update
  187.2 20.2 %all-reduce.5.cloned.1.call-done = bf16[1536,768]{1,0:T(8,128)(2,1)} async-done(((bf16[1536,768]{1,0:T(8,128)(2,1)}), bf16[1536,768]{1,0:T(8,128)(2,1)}) %all-reduce.5.cloned.1.call-update) | async-done | bytes 2359312 | tf_op jit(solution)/shard_map/psum | solution.py:100
  207.3 2.1 convert_element_type.71
  209.4 1.8 convolution_convert_fusion.1
  211.3 78.2 %all_to_all.11 = bf16[16,96,1024]{2,1,0:T(8,128)(2,1)S(1)} all-to-all(bf16[16,96,1024]{2,1,0:T(8,128)(2,1)S(1)} %bitcast.86), channel_id=1, replica_groups=mesh['groups'=1,'tm'=8,'expert'=2,'head'=2] {'tm','expert'}, dimensions={0} | all-to-all | bytes 6291456 | tf_op jit(solution)/shard_map/all_to_all | solution.py:13
  289.5 2.3 fusion.14
  (12 shorter events, 0.1 us)
Async XLA Ops:
  6.5 176.8 %copy-start = (bf16[1,1024,768]{2,1,0:T(8,128)(2,1)S(1)}, bf16[1,1024,768]{2,1,0:T(8,128)(2,1)}, u32[]{:S(2)}) copy-start(bf16[1,1024,768]{2,1,0:T(8,128)(2,1)} %param.20) | copy-start | bytes 4718596
  6.5 68.7 %copy-start.3 = (s32[1,1024]{1,0:T(1,128)S(1)}, s32[1,1024]{1,0:T(1,128)}, u32[]{:S(2)}) copy-start(s32[1,1024]{1,0:T(1,128)} %param.14) | copy-start | bytes 12292
  6.5 71.9 %all-gather.2.cloned.1.call-start = ((), (), s32[]{:S(2)}) async-start(), calls=%async_computation.2 | async-start | bytes 6291456 | tf_op jit(solution)/shard_map/all_gather | solution.py:63
  7.3 93.4 %all-reduce.3.cloned.1.call-start = ((), (), s32[]{:S(2)}) async-start(), calls=%async_computation.3 | async-start | bytes 1048576 | tf_op jit(solution)/shard_map/psum | solution.py:72
  78.4 3.0 %copy-start.1 = (bf16[1,128,1024]{2,1,0:T(8,128)(2,1)S(1)}, bf16[1,128,1024]{2,1,0:T(8,128)(2,1)}, u32[]{:S(2)}) copy-start(bf16[1,128,1024]{2,1,0:T(8,128)(2,1)} %param.15) | copy-start | bytes 786436
  78.5 4.1 %copy-start.2 = (f32[1,128,8]{1,2,0:T(8,128)S(1)}, f32[1,128,8]{1,2,0:T(8,128)}, u32[]{:S(2)}) copy-start(f32[1,128,8]{1,2,0:T(8,128)} %param.19) | copy-start | bytes 12292
  81.5 21.6 %copy-start.4 = (f32[1024]{0:T(1024)S(1)}, f32[1024]{0:T(1024)}, u32[]{:S(2)}) copy-start(f32[1024]{0:T(1024)} %param.17) | copy-start | bytes 12292
  82.5 124.8 %all-reduce.5.cloned.1.call-start = ((), (), s32[]{:S(2)}) async-start(), calls=%async_computation.4 | async-start | bytes 4718592 | tf_op jit(solution)/shard_map/psum | solution.py:100
  207.3 2.1 copy-start.5
Sparse Core Ops, SparseCore 0:
  8.9 59.4 all-gather.1
  82.6 17.9 all-reduce.2
  187.3 19.9 all-reduce.4
where the time goes:
time: 299 us; the launch traced here: 298 us
  blocking collectives  216 us (72%)
  waiting for transfers between devices  30.6 us (10%)
  other arithmetic  19.7 us (7%)
  matrix products  14.8 us (5%)
  between operations  13.3 us (4%)
  local copies, waits for them, and re-layouts  3.95 us (1%)
    all_to_all x2, blocking collectives, deliver(): lax.all_to_all(buffer, ('tm', 'expert'), split_axis=0, concat_axis=0, til...  156 us
    all_gather x1, blocking collectives, local(): key_blk = lax.all_gather(keys, 'tm', axis=1, tiled=True)[0]  32.9 us
    all_gather x1, blocking collectives, local(): value_blk = lax.all_gather(values, 'tm', axis=1, tiled=True)[0]  26.4 us
    psum x1, waiting for transfers between devices, local(): gate_up = lax.psum(block_gate, 'head').astype(jnp.float32)  20.2 us
    psum x1, waiting for transfers between devices, local(): lax.psum((partial_value + placed).astype(jnp.bfloat16), 'head')  9.66 us
    reduce_sum x1, other arithmetic, local(): jnp.sum(pair_match.reshape(expert_total * capacity, tokens, top_count).as...  8.38 us
  transfers between devices with their start and end apart: 3, of which 2 were waited for; matrix products, arithmetic and copies ran while one was open for 7% of the time, Pallas kernels for 0%

commit v1 on v0

--- a/solution.py
+++ b/solution.py
@@ -3,10 +3,13 @@
 import jax
 import jax.numpy as jnp
 from jax import lax
+from jax.experimental import pallas as pl
+from jax.experimental.pallas import tpu as pltpu
 from jax.sharding import PartitionSpec as P
 
 masked_score = -1e30
 epsilon = 1e-06
+MESH = pl.DeviceIdType.MESH
 
 
 def deliver(buffer):
@@ -118,6 +121,376 @@
     return layer_out[None]
 
 
+def fused_kernel(
+    q_ref,
+    k_ref,
+    v_ref,
+    seg_ref,
+    resid_ref,
+    ow_ref,
+    gain_ref,
+    routes_ref,
+    rw_ref,
+    wgu_ref,
+    wdn_ref,
+    out_ref,
+    kv,
+    coef,
+    attended,
+    core_send,
+    core_recv,
+    diag_send,
+    diag_recv,
+    projected,
+    squares,
+    hidden,
+    rows,
+    gu_other,
+    dn_other,
+    part_send,
+    part_recv,
+    y_send,
+    y_recv,
+    z_send,
+    z_recv,
+    kept,
+    kv_ss,
+    kv_rs,
+    coef_ss,
+    coef_rs,
+    row_ss,
+    row_rs,
+    w_ss,
+    w_rs,
+    att_ss,
+    att_rs,
+    mid_ss,
+    mid_rs,
+    part_ss,
+    part_rs,
+    y_ss,
+    y_rs,
+    z_ss,
+    z_rs,
+):
+    f32, bf16 = jnp.float32, jnp.bfloat16
+    tm = lax.axis_index("tm")
+    x = lax.axis_index("expert")
+    h = lax.axis_index("head")
+    z, y = tm // 2, tm % 2
+    far = [z, z + 1 - 2 * (z % 2), (z + 2) % 4, 3 - z]
+    to_y = {"tm": z * 2 + 1 - y}
+    to_z = [None] + [{"tm": far[d] * 2 + y} for d in (1, 2, 3)]
+    to_x = {"expert": 1 - x}
+    to_core = {"head": 1 - h}
+    to_diag = {"expert": 1 - x, "head": 1 - h}
+    tokens = q_ref.shape[0]
+    hd = k_ref.shape[1]
+    heads = q_ref.shape[1] // hd
+    width = resid_ref.shape[1]
+    ff = wdn_ref.shape[0]
+    experts = coef.shape[0] // 8
+
+    def remote(src, dst, ss, rs, dev):
+        return pltpu.make_async_remote_copy(
+            src_ref=src, dst_ref=dst, send_sem=ss, recv_sem=rs, device_id=dev, device_id_type=MESH
+        )
+
+    def spread(at, ss, rs):
+        copies = {1: remote(at(0), at(1), ss.at[1], rs.at[1], to_y)}
+        for d in (1, 2, 3):
+            copies[2 * d] = remote(at(0), at(2 * d), ss.at[2 * d], rs.at[2 * d], to_z[d])
+            copies[2 * d + 1] = remote(
+                at(2 * d), at(2 * d + 1), ss.at[2 * d + 1], rs.at[2 * d + 1], to_y
+            )
+        return copies
+
+    barrier = pltpu.get_barrier_semaphore()
+    peers = [to_y, to_z[1], to_z[2], to_z[3], to_x, to_core, to_diag]
+    for dev in peers:
+        pl.semaphore_signal(barrier, inc=1, device_id=dev, device_id_type=MESH)
+
+    kv[0, 0] = k_ref[...]
+    kv[0, 1] = v_ref[...]
+    lanes = lax.broadcasted_iota(jnp.int32, (tokens, 128), 1)
+    dense = jnp.zeros((tokens, 128), f32)
+    for k in range(routes_ref.shape[1]):
+        dense += jnp.where(lanes == routes_ref[:, k : k + 1], rw_ref[:, k : k + 1], 0.0)
+    coef[0:experts, :] = dense.T[0:experts, :]
+
+    pl.semaphore_wait(barrier, len(peers))
+
+    kv_at = lambda s: kv.at[s]
+    kv_copies = spread(kv_at, kv_ss, kv_rs)
+    coef_copies = spread(lambda s: coef.at[pl.ds(s * experts, experts)], coef_ss, coef_rs)
+    row_copies = spread(lambda s: rows.at[s], row_ss, row_rs)
+    for s in (1, 2, 4, 6):
+        kv_copies[s].start()
+    half = wgu_ref.shape[0] // 2
+    w_copies = [
+        remote(wgu_ref.at[pl.ds(0, half)], gu_other.at[pl.ds(0, half)], w_ss.at[0], w_rs.at[0], to_x),
+        remote(
+            wgu_ref.at[pl.ds(half, half)], gu_other.at[pl.ds(half, half)], w_ss.at[1], w_rs.at[1], to_x
+        ),
+        remote(wdn_ref, dn_other, w_ss.at[2], w_rs.at[2], to_x),
+    ]
+    w_copies[0].start()
+    for s in (1, 2, 4, 6):
+        coef_copies[s].start()
+    for d in (1, 2, 3):
+        kv_copies[2 * d].wait_recv()
+        kv_copies[2 * d + 1].start()
+    for d in (1, 2, 3):
+        coef_copies[2 * d].wait_recv()
+        coef_copies[2 * d + 1].start()
+    for s in (1, 3, 5, 7):
+        kv_copies[s].wait_recv()
+
+    own_ids = seg_ref[:, pl.ds(pl.multiple_of(tm * tokens, tokens), tokens)].astype(f32)
+    own_column = jnp.broadcast_to(own_ids, (tokens, tokens)).T
+    allowed = []
+    for s in range(8):
+        place = far[s // 2] * 2 + (y if s % 2 == 0 else 1 - y)
+        ids = seg_ref[:, pl.ds(pl.multiple_of(place * tokens, tokens), tokens)].astype(f32)
+        allowed.append(jnp.broadcast_to(ids, (tokens, tokens)) <= own_column)
+    allowed = jnp.concatenate(
+        [jnp.where(a, 0.0, masked_score) for a in allowed], axis=1
+    )
+    key_all = kv[:, 0].reshape(8 * tokens, hd)
+    value_all = kv[:, 1].reshape(8 * tokens, hd)
+    scale = 1.0 / math.sqrt(hd)
+    att_copies = []
+    for g in range(heads):
+        cols = pl.ds(g * hd, hd)
+        scores = lax.dot_general(
+            q_ref[:, cols], key_all, (((1,), (1,)), ((), ())), preferred_element_type=f32
+        )
+        scores = jnp.where(allowed < 0.0, masked_score, scores * scale)
+        top = jnp.max(scores, axis=1, keepdims=True)
+        probs = jnp.exp(scores - top)
+        total = jnp.sum(probs, axis=1, keepdims=True)
+        summed = jnp.dot(probs.astype(bf16), value_all, preferred_element_type=f32)
+        attended[x, :, cols] = (summed / total).astype(bf16)
+        if g % 2 == 1:
+            pair = pl.ds((g - 1) * hd, 2 * hd)
+            here = attended.at[x, :, pair]
+            copy = remote(here, here, att_ss.at[g // 2], att_rs.at[g // 2], to_x)
+            copy.start()
+            att_copies.append(copy)
+    for copy in att_copies:
+        copy.wait()
+
+    core_send[...] = jnp.dot(
+        attended[1 - h], ow_ref[...], preferred_element_type=f32
+    ).astype(bf16)
+    core_copy = remote(core_send, core_recv, mid_ss.at[0], mid_rs.at[0], to_core)
+    core_copy.start()
+    projected[...] = jnp.dot(attended[h], ow_ref[...], preferred_element_type=f32)
+    core_copy.wait()
+    projected[...] += core_recv[...].astype(f32)
+
+    @pl.when(x != h)
+    def _():
+        diag_send[...] = projected[...].astype(bf16)
+        diag_copy = remote(diag_send, diag_recv, mid_ss.at[1], mid_rs.at[1], to_diag)
+        diag_copy.start()
+        diag_copy.wait()
+        projected[...] = diag_recv[...].astype(f32)
+
+    w_copies[1].start()
+    w_copies[2].start()
+
+    hidden[...] = projected[...] + resid_ref[...].astype(f32)
+    own_sum = jnp.sum(hidden[...] * hidden[...], axis=1, keepdims=True)
+    squares[0] = jnp.broadcast_to(own_sum, (tokens, 128))
+    sq_copy = remote(squares.at[0], squares.at[1], mid_ss.at[2], mid_rs.at[2], to_core)
+    sq_copy.start()
+    sq_copy.wait()
+    mean = (squares[0][:, 0:1] + squares[1][:, 0:1]) * (1.0 / (2 * width))
+    rows[0] = (hidden[...] * lax.rsqrt(mean + epsilon) * gain_ref[...]).astype(bf16)
+    for s in (1, 2, 4, 6):
+        row_copies[s].start()
+    for s in (1, 3, 5, 7):
+        coef_copies[s].wait_recv()
+    by_token = coef[...].T
+
+    part_copies = [[None] * 8, [None] * 8]
+
+    def gate_up(s, which, weights):
+        part_send[which, s] = jnp.dot(
+            rows[s], weights[...], preferred_element_type=f32
+        ).astype(bf16)
+        copy = remote(
+            part_send.at[which, s],
+            part_recv.at[which, s],
+            part_ss.at[which, s],
+            part_rs.at[which, s],
+            to_core,
+        )
+        copy.start()
+        part_copies[which][s] = copy
+
+    gate_up(0, 0, wgu_ref)
+    for s in (1, 2, 3, 4, 5, 6, 7):
+        row_copies[s].wait_recv()
+        if s % 2 == 0:
+            row_copies[s + 1].start()
+        gate_up(s, 0, wgu_ref)
+
+    w_copies[0].wait_recv()
+    w_copies[1].wait_recv()
+    w_copies[2].wait_recv()
+    mine = tm * 2 + x
+    theirs = tm * 2 + 1 - x
+
+    def expert(s, which, weights, index):
+        part_copies[which][s].wait_recv()
+        both = part_send[which, s].astype(f32) + part_recv[which, s].astype(f32)
+        gate, up = both[:, :ff], both[:, ff:]
+        act = (gate / (1.0 + jnp.exp(-gate)) * up).astype(bf16)
+        down = jnp.dot(act, weights[...], preferred_element_type=f32).astype(bf16).astype(f32)
+        wanted = jnp.where(lanes == s * experts + index, by_token, 0.0)
+        return down * jnp.sum(wanted, axis=1, keepdims=True)
+
+    y_copies, z_copies = {}, {}
+
+    def finish(s):
+        mixed = expert(s, 0, wdn_ref, mine) + expert(s, 1, dn_other, theirs)
+        d = s // 2
+        if s % 2 == 1:
+            y_send[d] = mixed.astype(bf16)
+            copy = remote(y_send.at[d], y_recv.at[d], y_ss.at[d], y_rs.at[d], to_y)
+            copy.start()
+            y_copies[d] = copy
+        else:
+            kept[d] = mixed
+
+    def pass_on(d):
+        y_copies[d].wait_recv()
+        if d == 0:
+            kept[0] = kept[0] + y_recv[0].astype(f32)
+            return
+        z_send[d - 1] = (kept[d] + y_recv[d].astype(f32)).astype(bf16)
+        copy = remote(
+            z_send.at[d - 1], z_recv.at[d - 1], z_ss.at[d - 1], z_rs.at[d - 1], to_z[d]
+        )
+        copy.start()
+        z_copies[d] = copy
+
+    order = [7, 6, 5, 4, 3, 2, 1, 0]
+    gate_up(order[0], 1, gu_other)
+    for i, s in enumerate(order):
+        if i + 1 < 8:
+            gate_up(order[i + 1], 1, gu_other)
+        finish(s)
+        if s % 2 == 1 and s < 7:
+            pass_on(s // 2 + 1)
+    pass_on(0)
+    total = hidden[...] + kept[0]
+    for d in (3, 2, 1):
+        z_copies[d].wait_recv()
+        total += z_recv[d - 1].astype(f32)
+    out_ref[...] = total.astype(bf16)
+
+    for s in range(1, 8):
+        kv_copies[s].wait_send()
+        coef_copies[s].wait_send()
+        row_copies[s].wait_send()
+    for copy in w_copies:
+        copy.wait_send()
+    for which in range(2):
+        for s in range(8):
+            part_copies[which][s].wait_send()
+    for d in range(4):
+        y_copies[d].wait_send()
+    for d in (1, 2, 3):
+        z_copies[d].wait_send()
+
+
+def fused(
+    queries,
+    keys,
+    values,
+    segments,
+    resid,
+    output_weight,
+    norm_gain,
+    routes,
+    route_weights,
+    w_gu,
+    w_down,
+):
+    bf16, f32 = jnp.bfloat16, jnp.float32
+    tokens, width = resid.shape[1:]
+    hd = keys.shape[2]
+    ff = w_down.shape[1]
+    experts = lax.axis_size("tm") * lax.axis_size("expert")
+    block = (tokens, width)
+    dma = pltpu.SemaphoreType.DMA
+    out = pl.pallas_call(
+        fused_kernel,
+        out_shape=jax.ShapeDtypeStruct(block, bf16),
+        in_specs=[pl.BlockSpec(memory_space=pltpu.VMEM)] * 11,
+        out_specs=pl.BlockSpec(memory_space=pltpu.VMEM),
+        scratch_shapes=[
+            pltpu.VMEM((8, 2, tokens, hd), bf16),
+            pltpu.VMEM((8 * experts, tokens), f32),
+            pltpu.VMEM((2, tokens, queries.shape[2]), bf16),
+            pltpu.VMEM((tokens, output_weight.shape[1]), bf16),
+            pltpu.VMEM((tokens, output_weight.shape[1]), bf16),
+            pltpu.VMEM(block, bf16),
+            pltpu.VMEM(block, bf16),
+            pltpu.VMEM(block, f32),
+            pltpu.VMEM((2, tokens, 128), f32),
+            pltpu.VMEM(block, f32),
+            pltpu.VMEM((8,) + block, bf16),
+            pltpu.VMEM(w_gu.shape[1:], bf16),
+            pltpu.VMEM(w_down.shape[1:], bf16),
+            pltpu.VMEM((2, 8, tokens, 2 * ff), bf16),
+            pltpu.VMEM((2, 8, tokens, 2 * ff), bf16),
+            pltpu.VMEM((4,) + block, bf16),
+            pltpu.VMEM((4,) + block, bf16),
+            pltpu.VMEM((3,) + block, bf16),
+            pltpu.VMEM((3,) + block, bf16),
+            pltpu.VMEM((4,) + block, f32),
+            dma((8,)),
+            dma((8,)),
+            dma((8,)),
+            dma((8,)),
+            dma((8,)),
+            dma((8,)),
+            dma((3,)),
+            dma((3,)),
+            dma((4,)),
+            dma((4,)),
+            dma((3,)),
+            dma((3,)),
+            dma((2, 8)),
+            dma((2, 8)),
+            dma((4,)),
+            dma((4,)),
+            dma((3,)),
+            dma((3,)),
+        ],
+        compiler_params=pltpu.CompilerParams(
+            collective_id=0, has_side_effects=True, vmem_limit_bytes=56 * 2**20
+        ),
+    )(
+        queries[0],
+        keys[0],
+        values[0],
+        segments,
+        resid[0],
+        output_weight,
+        norm_gain[None],
+        routes[0],
+        route_weights[0],
+        w_gu[0],
+        w_down[0],
+    )
+    return out[None]
+
+
 def solution(mesh):
     placed = (
         P(("groups", "expert"), "tm", "head"),
@@ -132,8 +505,10 @@
         P(("tm", "expert"), "head", None),
         P(("tm", "expert"), None, "head"),
     )
+    sizes = mesh.shape
+    few = (sizes["tm"], sizes["expert"], sizes["head"]) == (8, 2, 2)
     return jax.shard_map(
-        local,
+        fused if few else local,
         mesh=mesh,
         in_specs=placed,
         out_specs=P(("groups", "expert"), "tm", "head"),

time: 299 us -> 115 us (0.38)
  blocking collectives: 216 us -> 0 us
  Pallas kernels: 0 us -> 111 us
  waiting for transfers between devices: 30.6 us -> 0 us
  other arithmetic: 19.7 us -> 0 us
  matrix products: 14.8 us -> 0 us
  between operations: 13.3 us -> 0.01 us
    all_to_all x2 -> x0, blocking collectives: 156 us -> none  [deliver(): lax.all_to_all(buffer, ('tm', 'expert'), split_axis=0, concat_axis=0, til...]
    pallas_call x0 -> x1, Pallas kernels: none -> 111 us  [fused(): pl.pallas_call(fused_kernel, out_shape=jax.ShapeDtypeStruct(block, bf16),...]
    all_gather x2 -> x0, blocking collectives: 59.4 us -> none  [the longest x1 32.9 us: local(): key_blk = lax.all_gather(keys, 'tm', axis=1, tiled=True)[0]]
    psum x2 -> x0, waiting for transfers between devices: 29.8 us -> none  [the longest x1 20.2 us: local(): gate_up = lax.psum(block_gate, 'head').astype(jnp.float32)]
    dot_general x7 -> x0, matrix products: 14.8 us -> none  [the longest x1 3.79 us: local(): jnp.dot(arrived_rows, w_gu[0], preferred_element_type=jnp.float32)]
    reduce_sum x4 -> x0, other arithmetic: 10.6 us -> none  [the longest x1 8.38 us: local(): jnp.sum(pair_match.reshape(expert_total * capacity, tokens, top_count).as...]
    another operation x4 -> x0, other arithmetic: 4.64 us -> none
    convert_element_type x4 -> x0, other arithmetic: 4.12 us -> none  [the longest x1 2.09 us: local(): gate_up = lax.psum(block_gate, 'head').astype(jnp.float32)]
  transfers between devices with their start and end apart: 3 -> 0, of which waited for: 2 -> 0; matrix products, arithmetic and copies ran while one was open for 7% -> 0% of each run, Pallas kernels for 0% -> 0%
where the time goes in v1:
time: 115 us
  Pallas kernels  111 us (97%)
  local copies, waits for them, and re-layouts  4.49 us (4%)
    pallas_call x1, Pallas kernels, fused(): pl.pallas_call(fused_kernel, out_shape=jax.ShapeDtypeStruct(block, bf16),...  111 us
    unnamed x3, local copies, waits for them, and re-layouts  4.49 us

profile of v1, /device:TPU:0, one launch (start us, length us, event | category | flops | bytes accessed | tf_op | source)
XLA Modules:
  0.0 115.0 jit_solution(11197461081118808016)
XLA Ops:
  0.0 1.4 %copy.12 = s32[1,128,8]{2,1,0:T(8,128)} copy(s32[1,128,8]{1,2,0:T(8,128)} %param.18) | data formatting | bytes 8192 | tf_op args[7]
  1.4 1.4 %copy.13 = f32[1,128,8]{2,1,0:T(8,128)} copy(f32[1,128,8]{1,2,0:T(8,128)} %param.19) | data formatting | bytes 8192 | tf_op args[8]
  2.8 110.5 %shard_map.109 = bf16[128,1024]{1,0:T(8,128)(2,1)} custom-call(bf16[128,1024]{1,0:T(8,128)(2,1)} %bitcast.15, bf16[128,128]{1,0:T(8,128)(2,1)} %bitcast.17, bf16[128,128]{1,0:T(8,128)(2,1)} %bitcast.18, s32[1,1024]{1,0:T(1,128)} %seg_ref.1, bf16[128,1024]{1,0:T(8,128)(2,1)} %bitcast.16, bf16[1024,1024]{1,0:T(8,128)(2,1)} %ow_ref.1, f32[1,1024]{1,0:T(1,128)} %bitcast.19, ...), custom_call_target="tpu_custom_call" | custom-call | tf_op jit(solution)/shard_map/pallas_call | solution.py:430
  113.4 1.7 %copy.15 = bf16[1,128,1024]{2,1,0:T(8,128)(2,1)} copy(bf16[1,128,1024]{2,1,0:T(8,128)(2,1)} %bitcast.11) | data formatting | bytes 524288

commit v2 on v0

--- a/solution.py
+++ b/solution.py
@@ -3,10 +3,13 @@
 import jax
 import jax.numpy as jnp
 from jax import lax
+from jax.experimental import pallas as pl
+from jax.experimental.pallas import tpu as pltpu
 from jax.sharding import PartitionSpec as P
 
 masked_score = -1e30
 epsilon = 1e-06
+MESH = pl.DeviceIdType.MESH
 
 
 def deliver(buffer):
@@ -118,6 +121,504 @@
     return layer_out[None]
 
 
+def fused_kernel(
+    q_ref,
+    k_ref,
+    v_ref,
+    seg_ref,
+    resid_hbm,
+    ow_hbm,
+    gain_ref,
+    routes_ref,
+    rw_ref,
+    wgu_hbm,
+    wdn_hbm,
+    out_ref,
+    kv,
+    coef,
+    attended,
+    core_send,
+    core_recv,
+    diag_send,
+    diag_recv,
+    projected,
+    squares,
+    hidden,
+    rows,
+    resid_ref,
+    ow_ref,
+    gu_own,
+    gu_other,
+    down,
+    acts,
+    part_send,
+    part_recv,
+    y_send,
+    y_recv,
+    z_send,
+    z_recv,
+    kept,
+    kv_ss,
+    kv_rs,
+    coef_ss,
+    coef_rs,
+    row_ss,
+    row_rs,
+    w_ss,
+    w_rs,
+    att_ss,
+    att_rs,
+    mid_ss,
+    mid_rs,
+    part_ss,
+    part_rs,
+    y_ss,
+    y_rs,
+    z_ss,
+    z_rs,
+    load_sems,
+):
+    f32, bf16 = jnp.float32, jnp.bfloat16
+    tm = lax.axis_index("tm")
+    x = lax.axis_index("expert")
+    h = lax.axis_index("head")
+    z, y = tm // 2, tm % 2
+    near = z - 1 + 2 * ((3 - z) // 3)
+    last = 3 * (1 - z // 2)
+    line = [near, 6 - z - near - last, last]
+    to_y = {"tm": z * 2 + 1 - y}
+    to_z = [{"tm": u * 2 + y} for u in line]
+    to_up, to_down = {"tm": tm + 2}, {"tm": tm - 2}
+    to_x = {"expert": 1 - x}
+    to_core = {"head": 1 - h}
+    to_diag = {"expert": 1 - x, "head": 1 - h}
+    tokens = q_ref.shape[0]
+    hd = k_ref.shape[1]
+    heads = q_ref.shape[1] // hd
+    width = resid_ref.shape[1]
+    ff = wdn_hbm.shape[0]
+    loads = [
+        pltpu.make_async_copy(src, dst, load_sems.at[i])
+        for i, (src, dst) in enumerate(
+            [
+                (ow_hbm, ow_ref),
+                (resid_hbm, resid_ref),
+                (wgu_hbm, gu_own),
+                (wdn_hbm, down.at[pl.ds(0, ff)]),
+            ]
+        )
+    ]
+    for load in loads:
+        load.start()
+    experts = coef.shape[0] // 8
+
+    def remote(src, dst, ss, rs, dev):
+        return pltpu.make_async_remote_copy(
+            src_ref=src, dst_ref=dst, send_sem=ss, recv_sem=rs, device_id=dev, device_id_type=MESH
+        )
+
+    class Spread:
+        def __init__(self, at, chunks, ss, rs):
+            self.at, self.chunks, self.ss, self.rs = at, chunks, ss, rs
+
+        def copies(self, u, c):
+            slot = 2 * u + y
+            here = self.at(slot, c)
+            rs = self.rs.at[slot, c]
+            return [
+                remote(here, here, self.ss.at[way, u, c], rs, dev)
+                for way, dev in enumerate((to_up, to_down, to_y))
+            ]
+
+        def send(self, u, c):
+            up, down, across = self.copies(u, c)
+            pl.when((z < 3) & (u <= z))(up.start)
+            pl.when((z > 0) & (u >= z))(down.start)
+            across.start()
+
+        def arrive(self, slot, c):
+            here = self.at(slot, c)
+            remote(here, here, self.ss.at[2, 0, c], self.rs.at[slot, c], to_y).wait_recv()
+
+        def begin(self):
+            for c in range(self.chunks):
+                self.send(z, c)
+
+        def relay(self, u, c):
+            self.arrive(2 * u + y, c)
+            self.send(u, c)
+
+        def finish(self):
+            for u in range(4):
+                for c in range(self.chunks):
+                    up, down, across = self.copies(u, c)
+                    pl.when((z < 3) & (u <= z))(up.wait_send)
+                    pl.when((z > 0) & (u >= z))(down.wait_send)
+                    across.wait_send()
+
+    class Direct(Spread):
+        def copies(self, u, c):
+            here = self.at(2 * u + y, c)
+            return remote(here, here, self.ss.at[2, u, c], self.rs.at[2 * u + y, c], to_y)
+
+        def sends(self):
+            here, rs = self.at(tm, 0), self.rs.at[tm, 0]
+            return [remote(here, here, self.ss.at[0, i, 0], rs, to_z[i]) for i in range(3)]
+
+        def begin(self):
+            self.copies(z, 0).start()
+            for copy in self.sends():
+                copy.start()
+
+        def send(self, u, c):
+            self.copies(u, c).start()
+
+        def finish(self):
+            for u in range(4):
+                self.copies(u, 0).wait_send()
+            for copy in self.sends():
+                copy.wait_send()
+
+    barrier = pltpu.get_barrier_semaphore()
+    peers = [to_y, to_x, to_core, to_diag] + to_z
+    for dev in peers:
+        pl.semaphore_signal(barrier, inc=1, device_id=dev, device_id_type=MESH)
+
+    kv[tm, 0] = k_ref[...]
+    kv[tm, 1] = v_ref[...]
+    lanes = lax.broadcasted_iota(jnp.int32, (tokens, 128), 1)
+    numbers = lax.broadcasted_iota(jnp.int32, (experts, tokens), 0)
+    dense = jnp.zeros((experts, tokens), f32)
+    for k in range(routes_ref.shape[0]):
+        dense += jnp.where(numbers == routes_ref[k : k + 1, :], rw_ref[k : k + 1, :], 0.0)
+    coef[pl.ds(tm * experts, experts), :] = dense
+
+    pl.semaphore_wait(barrier, len(peers))
+
+    kv_spread = Direct(lambda s, c: kv.at[s], 1, kv_ss, kv_rs)
+    coef_spread = Direct(lambda s, c: coef.at[pl.ds(s * experts, experts)], 1, coef_ss, coef_rs)
+    piece = tokens // row_rs.shape[1]
+    row_spread = Spread(
+        lambda s, c: rows.at[s, pl.ds(c * piece, piece)], row_rs.shape[1], row_ss, row_rs
+    )
+    kv_spread.begin()
+    gu_rows = wgu_hbm.shape[0] // 8
+    parts = 2
+    part = width // parts
+    dn_rows = ff // 2
+    w_parts = [
+        (wgu_hbm.at[pl.ds(i * gu_rows, gu_rows)], gu_other.at[pl.ds(i * gu_rows, gu_rows)])
+        for i in range(8)
+    ] + [
+        (
+            wdn_hbm.at[pl.ds(r * dn_rows, dn_rows), pl.ds(c * part, part)],
+            down.at[pl.ds(ff + r * dn_rows, dn_rows), pl.ds(c * part, part)],
+        )
+        for c in range(parts)
+        for r in range(2)
+    ]
+    w_copies = [
+        remote(src, dst, w_ss.at[i], w_rs.at[i], to_x) for i, (src, dst) in enumerate(w_parts)
+    ]
+    waiting = list(w_copies)
+
+    def some_weights(count):
+        for copy in waiting[:count]:
+            copy.start()
+        del waiting[:count]
+
+    some_weights(3)
+    coef_spread.begin()
+    for u in line:
+        kv_spread.relay(u, 0)
+    for u in line:
+        coef_spread.relay(u, 0)
+    kv_spread.arrive(tm + 1 - 2 * y, 0)
+    for u in line:
+        kv_spread.arrive(2 * u + 1 - y, 0)
+
+    own_ids = seg_ref[:, pl.ds(pl.multiple_of(tm * tokens, tokens), tokens)].astype(f32)
+    own_column = jnp.broadcast_to(own_ids, (tokens, tokens)).T
+    all_ids = jnp.broadcast_to(seg_ref[...].astype(f32), (tokens, 8 * tokens))
+    allowed = all_ids <= jnp.concatenate([own_column] * 8, axis=1)
+    key_all = kv[:, 0].reshape(8 * tokens, hd)
+    value_all = kv[:, 1].reshape(8 * tokens, hd)
+    scale = 1.0 / math.sqrt(hd)
+    pieces = row_spread.chunks
+    att_copies = {}
+    for c in range(pieces):
+        some = pl.ds(c * piece, piece)
+        allowed_here = allowed[c * piece : (c + 1) * piece]
+        for g in range(heads):
+            cols = pl.ds(g * hd, hd)
+            scores = lax.dot_general(
+                q_ref[some, cols], key_all, (((1,), (1,)), ((), ())), preferred_element_type=f32
+            )
+            scores = jnp.where(allowed_here, scores * scale, masked_score)
+            top = jnp.max(scores, axis=1, keepdims=True)
+            probs = jnp.exp(scores - top)
+            total = jnp.sum(probs, axis=1, keepdims=True)
+            summed = jnp.dot(probs.astype(bf16), value_all, preferred_element_type=f32)
+            attended[x, some, cols] = (summed / total).astype(bf16)
+            if g % 4 == 3:
+                here = attended.at[x, some, pl.ds((g - 3) * hd, 4 * hd)]
+                i = c, g // 4
+                att_copies[i] = remote(here, here, att_ss.at[i], att_rs.at[i], to_x)
+                att_copies[i].start()
+
+    def mid(c, i, src, dst, dev):
+        some = pl.ds(c * piece, piece)
+        return remote(src.at[some], dst.at[some], mid_ss.at[i, c], mid_rs.at[i, c], dev)
+
+    core_copies = [mid(c, 0, core_send, core_recv, to_core) for c in range(pieces)]
+    diag_copies = [mid(c, 1, diag_send, diag_recv, to_diag) for c in range(pieces)]
+    sq_copies = [mid(c, 2, squares.at[0], squares.at[1], to_core) for c in range(pieces)]
+    loads[0].wait()
+    for c in range(pieces):
+        some = pl.ds(c * piece, piece)
+        for i in range(2):
+            att_copies[c, i].wait()
+        core_send[some] = jnp.dot(
+            attended[1 - h, some], ow_ref[...], preferred_element_type=f32
+        ).astype(bf16)
+        core_copies[c].start()
+        projected[some] = jnp.dot(attended[h, some], ow_ref[...], preferred_element_type=f32)
+    some_weights(1)
+    for c in range(pieces):
+        some = pl.ds(c * piece, piece)
+        core_copies[c].wait()
+        projected[some] += core_recv[some].astype(f32)
+        diag_send[some] = projected[some].astype(bf16)
+        pl.when(x != h)(diag_copies[c].start)
+    some_weights(2)
+    loads[1].wait()
+    for c in range(pieces):
+        some = pl.ds(c * piece, piece)
+
+        @pl.when(x != h)
+        def _():
+            diag_copies[c].wait()
+            projected[some] = diag_recv[some].astype(f32)
+
+        full = projected[some] + resid_ref[some].astype(f32)
+        hidden[some] = full
+        own_sum = jnp.sum(full * full, axis=1, keepdims=True)
+        squares[0, some] = jnp.broadcast_to(own_sum, (piece, 128))
+        sq_copies[c].start()
+    for c in range(pieces):
+        some = pl.ds(c * piece, piece)
+        sq_copies[c].wait()
+        mean = (squares[0, some][:, 0:1] + squares[1, some][:, 0:1]) * (1.0 / (2 * width))
+        rows[tm, some] = (hidden[some] * lax.rsqrt(mean + epsilon) * gain_ref[...]).astype(bf16)
+        row_spread.send(z, c)
+    coef_spread.arrive(tm + 1 - 2 * y, 0)
+    for u in line:
+        coef_spread.arrive(2 * u + 1 - y, 0)
+    by_token = coef[...].T
+
+    def part_copy(s, which):
+        return remote(
+            part_send.at[which, s],
+            part_recv.at[which, s],
+            part_ss.at[which, s],
+            part_rs.at[which, s],
+            to_core,
+        )
+
+    def gate_up(s, which, weights):
+        part_send[which, s] = jnp.dot(
+            rows[s], weights[...], preferred_element_type=f32
+        ).astype(bf16)
+        part_copy(s, which).start()
+
+    loads[2].wait()
+    gate_up(tm, 0, gu_own)
+
+    def across(u):
+        for c in range(row_spread.chunks):
+            row_spread.arrive(2 * u + 1 - y, c)
+        gate_up(2 * u + 1 - y, 0, gu_own)
+
+    for i, u in enumerate(line):
+        for c in range(row_spread.chunks):
+            row_spread.relay(u, c)
+            some_weights(1)
+        gate_up(2 * u + y, 0, gu_own)
+        across(z if i == 0 else line[i - 1])
+    across(line[2])
+
+    for copy in w_copies[:8]:
+        copy.wait_recv()
+    inward = [line[2], line[1], line[0], z]
+    order = [2 * u + 1 - y for u in inward] + [2 * u + y for u in inward]
+    for s in order:
+        gate_up(s, 1, gu_other)
+
+    mine = [tm * 2 + x, tm * 2 + 1 - x]
+    for s in order:
+        for which in range(2):
+            part_copy(s, which).wait_recv()
+            both = part_send[which, s].astype(f32) + part_recv[which, s].astype(f32)
+            gate, up = both[:, :ff], both[:, ff:]
+            wanted = jnp.where(lanes == s * experts + mine[which], by_token, 0.0)
+            weight = jnp.sum(wanted, axis=1, keepdims=True)
+            acts[s, :, which * ff : (which + 1) * ff] = (
+                gate / (1.0 + jnp.exp(-gate)) * up * weight
+            ).astype(bf16)
+
+    def y_copy(u, c):
+        cols = pl.ds(c * part, part)
+        return remote(y_send.at[u, :, cols], y_recv.at[u, :, cols], y_ss.at[u, c], y_rs.at[u, c], to_y)
+
+    def z_copy(u, c, mine):
+        cols = pl.ds(c * part, part)
+        slot = z if mine else u
+        return remote(
+            z_send.at[u, :, cols],
+            z_recv.at[slot, :, cols],
+            z_ss.at[u, c],
+            z_rs.at[slot, c],
+            {"tm": u * 2 + y},
+        )
+
+    def pass_on(u, c):
+        cols = pl.ds(c * part, part)
+        y_copy(u, c).wait_recv()
+        z_send[u, :, cols] = (kept[u, :, cols] + y_recv[u, :, cols].astype(f32)).astype(bf16)
+        z_copy(u, c, True).start()
+
+    loads[3].wait()
+    for c in range(parts):
+        cols = pl.ds(c * part, part)
+        for copy in w_copies[8 + 2 * c : 10 + 2 * c]:
+            copy.wait_recv()
+        for i, s in enumerate(order):
+            u = inward[i % 4]
+            mixed = jnp.dot(acts[s], down[:, cols], preferred_element_type=f32)
+            if i >= 4:
+                kept[u, :, cols] = mixed
+                continue
+            y_send[u, :, cols] = mixed.astype(bf16)
+            y_copy(u, c).start()
+    for c in range(parts):
+        for u in inward[:3]:
+            pass_on(u, c)
+    for c in range(parts):
+        cols = pl.ds(c * part, part)
+        y_copy(z, c).wait_recv()
+        mixed = hidden[:, cols] + kept[z, :, cols] + y_recv[z, :, cols].astype(f32)
+        for u in inward[:3]:
+            z_copy(u, c, False).wait_recv()
+            mixed += z_recv[u, :, cols].astype(f32)
+        out_ref[:, cols] = mixed.astype(bf16)
+
+    for spread in (kv_spread, coef_spread, row_spread):
+        spread.finish()
+    for copy in w_copies:
+        copy.wait_send()
+    for s in range(8):
+        for which in range(2):
+            part_copy(s, which).wait_send()
+    for u in range(4):
+        for c in range(parts):
+            y_copy(u, c).wait_send()
+    for u in line:
+        for c in range(parts):
+            z_copy(u, c, True).wait_send()
+
+
+def fused(
+    queries,
+    keys,
+    values,
+    segments,
+    resid,
+    output_weight,
+    norm_gain,
+    routes,
+    route_weights,
+    w_gu,
+    w_down,
+):
+    bf16, f32 = jnp.bfloat16, jnp.float32
+    tokens, width = resid.shape[1:]
+    hd = keys.shape[2]
+    ff = w_down.shape[1]
+    experts = lax.axis_size("tm") * lax.axis_size("expert")
+    block = (tokens, width)
+    dma = pltpu.SemaphoreType.DMA
+    out = pl.pallas_call(
+        fused_kernel,
+        out_shape=jax.ShapeDtypeStruct(block, bf16),
+        in_specs=[
+            pl.BlockSpec(memory_space=pl.ANY if i in (4, 5, 9, 10) else pltpu.VMEM)
+            for i in range(11)
+        ],
+        out_specs=pl.BlockSpec(memory_space=pltpu.VMEM),
+        scratch_shapes=[
+            pltpu.VMEM((8, 2, tokens, hd), bf16),
+            pltpu.VMEM((8 * experts, tokens), f32),
+            pltpu.VMEM((2, tokens, queries.shape[2]), bf16),
+            pltpu.VMEM((tokens, output_weight.shape[1]), bf16),
+            pltpu.VMEM((tokens, output_weight.shape[1]), bf16),
+            pltpu.VMEM(block, bf16),
+            pltpu.VMEM(block, bf16),
+            pltpu.VMEM(block, f32),
+            pltpu.VMEM((2, tokens, 128), f32),
+            pltpu.VMEM(block, f32),
+            pltpu.VMEM((8,) + block, bf16),
+            pltpu.VMEM(block, bf16),
+            pltpu.VMEM(output_weight.shape, bf16),
+            pltpu.VMEM(w_gu.shape[1:], bf16),
+            pltpu.VMEM(w_gu.shape[1:], bf16),
+            pltpu.VMEM((2 * ff, width), bf16),
+            pltpu.VMEM((8, tokens, 2 * ff), bf16),
+            pltpu.VMEM((2, 8, tokens, 2 * ff), bf16),
+            pltpu.VMEM((2, 8, tokens, 2 * ff), bf16),
+            pltpu.VMEM((4,) + block, bf16),
+            pltpu.VMEM((4,) + block, bf16),
+            pltpu.VMEM((4,) + block, bf16),
+            pltpu.VMEM((4,) + block, bf16),
+            pltpu.VMEM((4,) + block, f32),
+            dma((3, 4, 1)),
+            dma((8, 1)),
+            dma((3, 4, 1)),
+            dma((8, 1)),
+            dma((3, 4, 2)),
+            dma((8, 2)),
+            dma((12,)),
+            dma((12,)),
+            dma((2, 2)),
+            dma((2, 2)),
+            dma((3, 2)),
+            dma((3, 2)),
+            dma((2, 8)),
+            dma((2, 8)),
+            dma((4, 2)),
+            dma((4, 2)),
+            dma((4, 2)),
+            dma((4, 2)),
+            dma((4,)),
+        ],
+        compiler_params=pltpu.CompilerParams(
+            collective_id=0, has_side_effects=True, vmem_limit_bytes=56 * 2**20
+        ),
+    )(
+        queries[0],
+        keys[0],
+        values[0],
+        segments,
+        resid[0],
+        output_weight,
+        norm_gain[None],
+        routes[0].T,
+        route_weights[0].T,
+        w_gu[0],
+        w_down[0],
+    )
+    return out[None]
+
+
 def solution(mesh):
     placed = (
         P(("groups", "expert"), "tm", "head"),
@@ -132,8 +633,10 @@
         P(("tm", "expert"), "head", None),
         P(("tm", "expert"), None, "head"),
     )
+    sizes = mesh.shape
+    few = (sizes["tm"], sizes["expert"], sizes["head"]) == (8, 2, 2)
     return jax.shard_map(
-        local,
+        fused if few else local,
         mesh=mesh,
         in_specs=placed,
         out_specs=P(("groups", "expert"), "tm", "head"),

time: 299 us -> 100 us (0.33)
  blocking collectives: 216 us -> 0 us
  Pallas kernels: 0 us -> 98.5 us
  waiting for transfers between devices: 30.6 us -> 0 us
  other arithmetic: 19.7 us -> 0 us
  matrix products: 14.8 us -> 0 us
  between operations: 13.3 us -> 0.01 us
    all_to_all x2 -> x0, blocking collectives: 156 us -> none  [deliver(): lax.all_to_all(buffer, ('tm', 'expert'), split_axis=0, concat_axis=0, til...]
    pallas_call x0 -> x1, Pallas kernels: none -> 98.5 us  [fused(): pl.pallas_call(fused_kernel, out_shape=jax.ShapeDtypeStruct(block, bf16),...]
    all_gather x2 -> x0, blocking collectives: 59.4 us -> none  [the longest x1 32.9 us: local(): key_blk = lax.all_gather(keys, 'tm', axis=1, tiled=True)[0]]
    psum x2 -> x0, waiting for transfers between devices: 29.8 us -> none  [the longest x1 20.2 us: local(): gate_up = lax.psum(block_gate, 'head').astype(jnp.float32)]
    dot_general x7 -> x0, matrix products: 14.8 us -> none  [the longest x1 3.79 us: local(): jnp.dot(arrived_rows, w_gu[0], preferred_element_type=jnp.float32)]
    reduce_sum x4 -> x0, other arithmetic: 10.6 us -> none  [the longest x1 8.38 us: local(): jnp.sum(pair_match.reshape(expert_total * capacity, tokens, top_count).as...]
    another operation x4 -> x0, other arithmetic: 4.64 us -> none
    convert_element_type x4 -> x0, other arithmetic: 4.12 us -> none  [the longest x1 2.09 us: local(): gate_up = lax.psum(block_gate, 'head').astype(jnp.float32)]
  transfers between devices with their start and end apart: 3 -> 0, of which waited for: 2 -> 0; matrix products, arithmetic and copies ran while one was open for 7% -> 0% of each run, Pallas kernels for 0% -> 0%
where the time goes in v2:
time: 100 us
  Pallas kernels  98.5 us (98%)
  local copies, waits for them, and re-layouts  1.67 us (2%)
    pallas_call x1, Pallas kernels, fused(): pl.pallas_call(fused_kernel, out_shape=jax.ShapeDtypeStruct(block, bf16),...  98.5 us

profile of v2, /device:TPU:0, one launch (start us, length us, event | category | flops | bytes accessed | tf_op | source)
XLA Modules:
  0.0 100.2 jit_solution(14152610998266775213)
XLA Ops:
  0.0 98.5 %shard_map.109 = bf16[128,1024]{1,0:T(8,128)(2,1)} custom-call(bf16[128,1024]{1,0:T(8,128)(2,1)} %bitcast.17, bf16[128,128]{1,0:T(8,128)(2,1)} %bitcast.19, bf16[128,128]{1,0:T(8,128)(2,1)} %bitcast.20, s32[1,1024]{1,0:T(1,128)} %seg_ref.1, bf16[128,1024]{1,0:T(8,128)(2,1)} %bitcast.18, bf16[1024,1024]{1,0:T(8,128)(2,1)} %ow_hbm.1, f32[1,1024]{1,0:T(1,128)} %bitcast.21, ...), custom_call_target="tpu_custom_call" | custom-call | tf_op jit(solution)/shard_map/pallas_call | solution.py:550
  98.5 1.7 %copy.13 = bf16[1,128,1024]{2,1,0:T(8,128)(2,1)} copy(bf16[1,128,1024]{2,1,0:T(8,128)(2,1)} %bitcast.15) | data formatting | bytes 524288

commit v3 on v2

--- a/solution.py
+++ b/solution.py
@@ -183,9 +183,9 @@
     x = lax.axis_index("expert")
     h = lax.axis_index("head")
     z, y = tm // 2, tm % 2
-    near = z - 1 + 2 * ((3 - z) // 3)
+    first = z - 1 + 2 * ((3 - z) // 3)
     last = 3 * (1 - z // 2)
-    line = [near, 6 - z - near - last, last]
+    line = [first, 6 - z - first - last, last]
     to_y = {"tm": z * 2 + 1 - y}
     to_z = [{"tm": u * 2 + y} for u in line]
     to_up, to_down = {"tm": tm + 2}, {"tm": tm - 2}
@@ -383,14 +383,14 @@
         ).astype(bf16)
         core_copies[c].start()
         projected[some] = jnp.dot(attended[h, some], ow_ref[...], preferred_element_type=f32)
-    some_weights(1)
+    some_weights(0)
     for c in range(pieces):
         some = pl.ds(c * piece, piece)
         core_copies[c].wait()
         projected[some] += core_recv[some].astype(f32)
         diag_send[some] = projected[some].astype(bf16)
         pl.when(x != h)(diag_copies[c].start)
-    some_weights(2)
+    some_weights(6)
     loads[1].wait()
     for c in range(pieces):
         some = pl.ds(c * piece, piece)
@@ -445,17 +445,11 @@
             some_weights(1)
         gate_up(2 * u + y, 0, gu_own)
         across(z if i == 0 else line[i - 1])
-    across(line[2])
-
-    for copy in w_copies[:8]:
-        copy.wait_recv()
-    inward = [line[2], line[1], line[0], z]
-    order = [2 * u + 1 - y for u in inward] + [2 * u + y for u in inward]
-    for s in order:
-        gate_up(s, 1, gu_other)
+    some_weights(12)
 
     mine = [tm * 2 + x, tm * 2 + 1 - x]
-    for s in order:
+
+    def activate(s):
         for which in range(2):
             part_copy(s, which).wait_recv()
             both = part_send[which, s].astype(f32) + part_recv[which, s].astype(f32)
@@ -465,6 +459,18 @@
             acts[s, :, which * ff : (which + 1) * ff] = (
                 gate / (1.0 + jnp.exp(-gate)) * up * weight
             ).astype(bf16)
+
+    for copy in w_copies[:8]:
+        copy.wait_recv()
+    near, middle, distant = line
+    late = 2 * distant + 1 - y
+    early = [2 * u + 1 - y for u in (middle, near, z)] + [
+        2 * u + y for u in (middle, near, distant, z)
+    ]
+    for s in early:
+        gate_up(s, 1, gu_other)
+    for s in early[:2]:
+        activate(s)
 
     def y_copy(u, c):
         cols = pl.ds(c * part, part)
@@ -487,27 +493,48 @@
         z_send[u, :, cols] = (kept[u, :, cols] + y_recv[u, :, cols].astype(f32)).astype(bf16)
         z_copy(u, c, True).start()
 
+    def down_dot(s, cols):
+        return jnp.dot(acts[s], down[:, cols], preferred_element_type=f32)
+
+    def give(u, c):
+        cols = pl.ds(c * part, part)
+        y_send[u, :, cols] = down_dot(2 * u + 1 - y, cols).astype(bf16)
+        y_copy(u, c).start()
+
+    def keep(u, c):
+        cols = pl.ds(c * part, part)
+        kept[u, :, cols] = down_dot(2 * u + y, cols)
+
     loads[3].wait()
-    for c in range(parts):
-        cols = pl.ds(c * part, part)
-        for copy in w_copies[8 + 2 * c : 10 + 2 * c]:
-            copy.wait_recv()
-        for i, s in enumerate(order):
-            u = inward[i % 4]
-            mixed = jnp.dot(acts[s], down[:, cols], preferred_element_type=f32)
-            if i >= 4:
-                kept[u, :, cols] = mixed
-                continue
-            y_send[u, :, cols] = mixed.astype(bf16)
-            y_copy(u, c).start()
-    for c in range(parts):
-        for u in inward[:3]:
-            pass_on(u, c)
+    for copy in w_copies[8:10]:
+        copy.wait_recv()
+    give(middle, 0)
+    give(near, 0)
+    for s in early[2:]:
+        activate(s)
+    across(distant)
+    gate_up(late, 1, gu_other)
+    activate(late)
+    give(distant, 0)
+    give(z, 0)
+    for u in (middle, near, distant, z):
+        keep(u, 0)
+    pass_on(middle, 0)
+    for copy in w_copies[10:12]:
+        copy.wait_recv()
+    for u in (distant, middle, near, z):
+        give(u, 1)
+    pass_on(near, 0)
+    for u in (distant, middle, near, z):
+        keep(u, 1)
+    pass_on(distant, 0)
+    for u in (distant, middle, near):
+        pass_on(u, 1)
     for c in range(parts):
         cols = pl.ds(c * part, part)
         y_copy(z, c).wait_recv()
         mixed = hidden[:, cols] + kept[z, :, cols] + y_recv[z, :, cols].astype(f32)
-        for u in inward[:3]:
+        for u in line:
             z_copy(u, c, False).wait_recv()
             mixed += z_recv[u, :, cols].astype(f32)
         out_ref[:, cols] = mixed.astype(bf16)

time: 100 us -> 97.3 us (0.973)
  Pallas kernels: 98.5 us -> 95.4 us
    pallas_call x1, Pallas kernels: 98.5 us -> 95.4 us  [fused(): pl.pallas_call(fused_kernel, out_shape=jax.ShapeDtypeStruct(block, bf16),...]
where the time goes in v3:
time: 97.3 us; the launch traced here: 97.1 us
  Pallas kernels  95.4 us (98%)
  local copies, waits for them, and re-layouts  1.67 us (2%)
    pallas_call x1, Pallas kernels, fused(): pl.pallas_call(fused_kernel, out_shape=jax.ShapeDtypeStruct(block, bf16),...  95.4 us

profile of v3, /device:TPU:0, one launch (start us, length us, event | category | flops | bytes accessed | tf_op | source)
XLA Modules:
  0.0 97.1 jit_solution(7576854695787517748)
XLA Ops:
  0.0 95.4 %shard_map.109 = bf16[128,1024]{1,0:T(8,128)(2,1)} custom-call(bf16[128,1024]{1,0:T(8,128)(2,1)} %bitcast.17, bf16[128,128]{1,0:T(8,128)(2,1)} %bitcast.19, bf16[128,128]{1,0:T(8,128)(2,1)} %bitcast.20, s32[1,1024]{1,0:T(1,128)} %seg_ref.1, bf16[128,1024]{1,0:T(8,128)(2,1)} %bitcast.18, bf16[1024,1024]{1,0:T(8,128)(2,1)} %ow_hbm.1, f32[1,1024]{1,0:T(1,128)} %bitcast.21, ...), custom_call_target="tpu_custom_call" | custom-call | tf_op jit(solution)/shard_map/pallas_call | solution.py:577
  95.4 1.7 %copy.13 = bf16[1,128,1024]{2,1,0:T(8,128)(2,1)} copy(bf16[1,128,1024]{2,1,0:T(8,128)(2,1)} %bitcast.15) | data formatting | bytes 524288
